TPU v7x, 256 devices: a whole 4x4x8 slice. The times are simulated.
256 devices in a mesh: row: 8 (over z), col: 32 (over x, y, core).
Axes of the slice: x: 4, y: 4, z: 8, core: 2. Of those that a mesh axis runs over, the one named last changes fastest.
Arguments:
- gradient: bfloat16 [8192, 53248], P('row', 'col'), may hold values from -6 to 6
- momentum: bfloat16 [8192, 53248], P('row', 'col'), may hold values from -8 to 8
- right_factor: bfloat16 [53248, 512], P('col'), may hold values from -0.02734375 to 0.02734375
Outputs:
- momentum_next: bfloat16 [8192, 53248], P('row', 'col')
- right_next: bfloat16 [53248, 512], P('col')
- update: bfloat16 [8192, 53248], P('row', 'col')
All inputs are finite; a program needn't handle non-finite values.
Results may differ from a plain program's by a relative error of at most 0.015.
Values may be sent and summed in bfloat16 or wider, within the bound.
No kernel may reach another device: no remote copies, remote signals or barrier semaphores. Data moves between devices by JAX's collectives and lax.ppermute only.
A program may use at most 64 MiB of HBM per device.

v0:
```python
import jax
import jax.numpy as jnp
from jax import lax
from jax.experimental import pallas as pl
from jax.experimental.pallas import tpu as pltpu
from jax.sharding import Mesh, PartitionSpec as P

HI = lax.Precision.HIGHEST
TILE = 8


def diag_inverse(block):
    n = block.shape[0]
    tiles = n // TILE
    shape = (TILE, n)
    row = lax.broadcasted_iota(jnp.int32, shape, 0)
    lane = lax.broadcasted_iota(jnp.int32, shape, 1)
    s = [block[t * TILE:(t + 1) * TILE, :] for t in range(tiles)]
    x = [jnp.where(lane == row + t * TILE, 1.0, 0.0) for t in range(tiles)]
    spread = lambda v, i: jnp.broadcast_to(v[i:i + 1, :], shape)
    for p in range(tiles):
        rest = range(p + 1, tiles)
        col = [
            {t: jnp.broadcast_to(s[t][:, p * TILE + b:p * TILE + b + 1], shape) for t in range(p, tiles)}
            for b in range(TILE)
        ]
        for j in range(TILE):
            inv = lax.rsqrt(spread(col[j][p], j))
            low = {t: col[j][t] * inv for t in range(p, tiles)}
            mult = jnp.where(row > j, low[p], 0.0)
            keep = jnp.where(row == j, inv, 1.0)
            for b in range(j + 1, TILE):
                u = spread(low[p], b)
                for t in range(p, tiles):
                    col[b][t] = col[b][t] - low[t] * u
            srow = spread(s[p], j) * inv
            xrow = spread(x[p], j) * inv
            s[p] = s[p] * keep - mult * srow
            x[p] = x[p] * keep - mult * xrow
            for t in rest:
                s[t] = s[t] - low[t] * srow
                x[t] = x[t] - low[t] * xrow
    return jnp.concatenate(x, axis=0)


def chol_kernel(gram_ref, inv_ref, work):
    n = gram_ref.shape[0]
    nb = 128
    work[...] = gram_ref[...]
    inv_ref[...] = jnp.zeros((n, n), jnp.float32)
    dot = lambda a, b: jnp.dot(a, b, precision=HI, preferred_element_type=jnp.float32)

    def finish(o, d):
        after = o + nb
        here = slice(o, after)
        inv_ref[here, here] = d
        if o:
            inv_ref[here, :o] = dot(d, inv_ref[here, :o])
        if after < n:
            u = dot(d, work[here, after:])
            ut = u.T
            work[after:, after:] = work[after:, after:] - dot(ut, u)
            inv_ref[after:, :after] = inv_ref[after:, :after] - dot(ut, inv_ref[here, :after])

    def step(k, carry):
        o = pl.multiple_of(k * nb, nb)
        d = diag_inverse(work[pl.ds(o, nb), pl.ds(o, nb)])
        for which in range(n // nb):
            pl.when(k == which)(lambda: finish(which * nb, d))
        return carry

    lax.fori_loop(0, n // nb, step, 0)

def chol_inverse(gram):
    n = gram.shape[0]
    return pl.pallas_call(
        chol_kernel,
        out_shape=jax.ShapeDtypeStruct((n, n), jnp.float32),
        in_specs=[pl.BlockSpec(memory_space=pltpu.VMEM)],
        out_specs=pl.BlockSpec(memory_space=pltpu.VMEM),
        scratch_shapes=[pltpu.VMEM((n, n), jnp.float32)],
        compiler_params=pltpu.CompilerParams(vmem_limit_bytes=16 * 1024 * 1024),
        cost_estimate=pl.CostEstimate(flops=20 * 10**9, bytes_accessed=8 * n * n, transcendentals=0),
    )(gram)


CHIPS = ("x", "y")
VMEM = 16 * 1024 * 1024
TN = (((0,), (0,)), ((), ()))
NT = (((1,), (1,)), ((), ()))


def call(kernel, out_shape, grid, in_specs, out_specs, scratch=(), flops=0, moved=0, scalars=1, vmem=VMEM):
    return pl.pallas_call(
        kernel,
        out_shape=out_shape,
        grid_spec=pltpu.PrefetchScalarGridSpec(
            num_scalar_prefetch=scalars, grid=grid, in_specs=in_specs, out_specs=out_specs, scratch_shapes=list(scratch)
        ),
        compiler_params=pltpu.CompilerParams(vmem_limit_bytes=vmem),
        cost_estimate=pl.CostEstimate(flops=flops, bytes_accessed=moved, transcendentals=0),
    )


def slab_kernel(place_ref, part_a, part_b, left_a, left_b, out_ref, scratch):
    width = out_ref.shape[0]
    scratch[...] = lax.dot_general(
        part_a[...], left_a[...], TN, precision=HI, preferred_element_type=jnp.float32
    ) + lax.dot_general(part_b[...], left_b[...], TN, precision=HI, preferred_element_type=jnp.float32)
    start = pl.multiple_of(lax.rem(place_ref[0], 128 // width) * width, width)
    out_ref[...] = scratch[pl.ds(start, width), :]


def gram_slab(place, width, left_a, left_b):
    rows, rank = left_a.shape
    part = pl.BlockSpec((rows, 128), lambda i, p: (0, p[0] // (128 // width)))
    whole = pl.BlockSpec((rows, rank), lambda i, p: (0, 0))
    return call(
        slab_kernel,
        jax.ShapeDtypeStruct((width, rank), jnp.float32),
        (1,),
        [part, part, whole, whole],
        pl.BlockSpec((width, rank), lambda i, p: (0, 0)),
        [pltpu.VMEM((128, rank), jnp.float32)],
        flops=24 * rows * 128 * rank,
        moved=10 * rows * rank,
    )(place.reshape(1), left_a, left_b, left_a, left_b)


def last_kernel(factor, orth_ref, blended_ref, right_ref, colsq_ref, momentum_ref, next_ref, update_ref):
    @pl.when(pl.program_id(0) == 0)
    def _():
        scale = 1.0 / jnp.sqrt(colsq_ref[...] + 1e-06)
        next_ref[...] = (right_ref[...].astype(jnp.float32) * scale).astype(jnp.bfloat16)

    correction = lax.dot_general(orth_ref[...], right_ref[...], NT, preferred_element_type=jnp.float32)
    momentum_ref[...] = (blended_ref[...].astype(jnp.float32) - 0.1 * correction).astype(jnp.bfloat16)
    product = lax.dot_general(orth_ref[...], next_ref[...], NT, preferred_element_type=jnp.float32)
    update_ref[...] = (factor * product).astype(jnp.bfloat16)


def last_products(factor, left_orth, blended, right_bf, colsq):
    rows, cols = blended.shape
    rank = left_orth.shape[1]
    tile = 256
    block = pl.BlockSpec((tile, cols), lambda i: (i, 0))
    whole = pl.BlockSpec((cols, rank), lambda i: (0, 0))
    big = jax.ShapeDtypeStruct((rows, cols), jnp.bfloat16)
    return call(
        lambda *refs: last_kernel(factor, *refs),
        (big, jax.ShapeDtypeStruct((cols, rank), jnp.bfloat16), big),
        (rows // tile,),
        [pl.BlockSpec((tile, rank), lambda i: (i, 0)), block, whole, pl.BlockSpec((1, rank), lambda i: (0, 0))],
        [block, whole, block],
        flops=4 * rows * cols * rank,
        moved=6 * rows * cols + 4 * cols * rank + 2 * rows * rank,
        scalars=0,
        vmem=60 * 1024 * 1024,
    )(left_orth, blended, right_bf, colsq)


def three_terms(value):
    high = lax.reduce_precision(value, 8, 7)
    rest = value - high
    mid = lax.reduce_precision(rest, 8, 7)
    return [t.astype(jnp.bfloat16) for t in (high, mid, rest - mid)]


def swap_cores(value):
    return lax.ppermute(value, "c", [(0, 1), (1, 0)])


def spread_over(value, axes, parts):
    many = jnp.broadcast_to(value[None], (parts,) + value.shape)
    return lax.all_to_all(many, axes, 0, 0, tiled=True)


def gather_over_chips(value, chips):
    return spread_over(value, CHIPS, chips).reshape(chips * value.shape[0], value.shape[1])


def per_device(gradient, momentum, right_factor):
    rows_dev, cols_dev = gradient.shape
    rank = right_factor.shape[1]
    chips = lax.axis_size("x") * lax.axis_size("y")
    depth = lax.axis_size("z")
    core = lax.axis_index("c")
    place = (core * lax.axis_size("x") + lax.axis_index("x")) * lax.axis_size("y") + lax.axis_index("y")
    blended = (momentum.astype(jnp.float32) + gradient.astype(jnp.float32)).astype(jnp.bfloat16)
    half = rows_dev // 2
    part_b, part_a = (
        jnp.dot(
            lax.dynamic_slice_in_dim(blended, h * half, half),
            right_factor,
            preferred_element_type=jnp.float32,
        )
        for h in (1 - core, core)
    )
    part_a = lax.optimization_barrier(part_a)
    pair = (part_a + swap_cores(part_b)).reshape(chips, rows_dev // (2 * chips), rank)
    shard = jnp.sum(lax.all_to_all(pair, CHIPS, 0, 0, tiled=True), axis=0)
    left_a = gather_over_chips(shard, chips)
    left_b = swap_cores(left_a)
    left = lax.dynamic_update_slice(jnp.zeros((rows_dev, rank), jnp.float32), left_a, (core * half, 0))
    left = lax.dynamic_update_slice(left, left_b, ((1 - core) * half, 0))
    wide = sum(
        lax.dot_general(blended, t, TN, preferred_element_type=jnp.float32) for t in three_terms(left)
    )
    wide = lax.psum_scatter(wide, "z", scatter_dimension=0, tiled=True)
    slab = gram_slab(place, rank // (2 * chips), left_a, left_b)
    slab = jnp.sum(spread_over(slab, "z", depth), axis=0)
    mine = gather_over_chips(slab, chips)
    other = swap_cores(mine)
    gram = jnp.concatenate([jnp.where(core == 0, mine, other), jnp.where(core == 0, other, mine)])
    inverse = chol_inverse(gram)
    right = lax.dot_general(wide, inverse, NT, precision=HI, preferred_element_type=jnp.float32)
    colsq = jnp.sum(right * right, axis=0)
    right_bf = lax.all_gather(right.astype(jnp.bfloat16), "z", axis=0, tiled=True)
    left_orth = lax.dot_general(left, inverse, NT, precision=HI, preferred_element_type=jnp.float32).astype(jnp.bfloat16)
    colsq = colsq.reshape(rank // 128, 128)
    colsq = jnp.sum(spread_over(colsq, ("x", "y", "c"), 2 * chips), axis=0)
    colsq = jnp.sum(spread_over(colsq, "z", depth), axis=0).reshape(1, rank)
    factor = (rows_dev * depth * cols_dev * 2 * chips / rank) ** 0.5
    return last_products(factor, left_orth, blended, right_bf, colsq)


def solution(mesh):
    fine = Mesh(mesh.devices.reshape(8, 4, 4, 2), ("z", "x", "y", "c"))
    col = ("x", "y", "c")
    return jax.shard_map(
        per_device,
        mesh=fine,
        in_specs=(P("z", col), P("z", col), P(col, None)),
        out_specs=(P("z", col), P(col, None), P("z", col)),
        check_vma=False,
    )
```

profile of v0, /device:TPU:96, one launch (start us, length us, event | category | flops | bytes accessed | tf_op | source)
XLA Modules:
  0.0 182.2 jit_solution(1441413053870140825)
XLA Ops:
  7.2 3.9 %add_convert_fusion.refs_1_ = bf16[1024,1664]{1,0:T(8,128)(2,1)S(1)} fusion(bf16[1024,1664]{1,0:T(8,128)(2,1)} %param.3, bf16[1024,1664]{1,0:T(8,128)(2,1)} %param.4), kind=kLoop, calls=%fused_computation | loop fusion | flops 6815744 | bytes 10223616 | tf_op jit(solution)/shard_map/convert_element_type | solution.py:189
  11.2 2.1 %fusion.1 = f32[512,512]{1,0:T(8,128)} fusion(bf16[1664,512]{1,0:T(8,128)(2,1)S(1)} %copy-done, bf16[1024,1664]{1,0:T(8,128)(2,1)S(1)} %add_convert_fusion.refs_1_, s32[]{:T(128)S(6)} %select_n.21), kind=kOutput, calls=%fused_computation.7 | convolution fusion | flops 872415232 | bytes 4456452 | tf_op jit(solution)/shard_map/dot_general | solution.py:192
  13.3 2.6 %fusion.3 = f32[512,512]{1,0:T(8,128)S(1)} fusion(bf16[1664,512]{1,0:T(8,128)(2,1)S(1)} %copy-done, bf16[1024,1664]{1,0:T(8,128)(2,1)} %copy-done.4, s32[]{:T(128)S(6)} %select_n.20), kind=kOutput, calls=%fused_computation.9 | convolution fusion | flops 872415232 | bytes 4456452 | tf_op jit(solution)/shard_map/dot_general | solution.py:192
  16.4 24.3 %all_to_all.30 = f32[16,32,512]{2,1,0:T(8,128)S(1)} all-to-all(f32[16,32,512]{2,1,0:T(8,128)S(1)} %bitcast.21), channel_id=1, replica_groups=mesh['z'=8,'x'=4,'y'=4,'c'=2] {'x','y'}, dimensions={0} | all-to-all | bytes 2097152 | tf_op jit(solution)/shard_map/all_to_all | solution.py:201
  40.9 19.6 %all_to_all.31 = f32[16,32,512]{2,1,0:T(8,128)S(1)} all-to-all(f32[16,32,512]{2,1,0:T(8,128)S(1)} %broadcast_in_dim.15), channel_id=1, replica_groups=mesh['z'=8,'x'=4,'y'=4,'c'=2] {'x','y'}, dimensions={0} | all-to-all | bytes 2097152 | tf_op jit(solution)/shard_map/all_to_all | solution.py:175
  60.9 2.3 %collective-permute-done.1.part_b.left_b = f32[512,512]{1,0:T(8,128)S(1)} collective-permute-done((f32[512,512]{1,0:T(8,128)S(1)}, f32[512,512]{1,0:T(8,128)S(1)}, u32[]{:S(2)}, u32[]{:S(2)}) %collective-permute-start.1) | collective-permute-done | bytes 1048608 | tf_op jit(solution)/shard_map/ppermute | solution.py:170
  63.3 1.0 copy-done.1
  64.2 2.0 %fusion.10 = f32[1664,512]{1,0:T(8,128)S(1)} fusion(bf16[1024,1664]{1,0:T(8,128)(2,1)S(1)} %copy-done.5, f32[1024,512]{1,0:T(8,128)S(1)} %constant_dynamic-update-slice_fusion), kind=kOutput, calls=%fused_computation.14 | convolution fusion | flops 1746927616 | bytes 8912896 | tf_op jit(solution)/shard_map/dot_general | solution.py:207
  66.2 2.0 %fusion.9 = f32[1664,512]{1,0:T(8,128)S(1)} fusion(bf16[1024,1664]{1,0:T(8,128)(2,1)S(1)} %copy-done.5, f32[1024,512]{1,0:T(8,128)S(1)} %constant_dynamic-update-slice_fusion), kind=kOutput, calls=%fused_computation.13 | convolution fusion | flops 1745879040 | bytes 8912896 | tf_op jit(solution)/shard_map/dot_general | solution.py:207
  68.2 3.8 %add_add_fusion = f32[1664,512]{1,0:T(8,128)} fusion(f32[1664,512]{1,0:T(8,128)S(1)} %fusion.9, f32[1664,512]{1,0:T(8,128)S(1)} %fusion.10, bf16[1024,1664]{1,0:T(8,128)(2,1)S(1)} %copy-done.5, f32[1024,512]{1,0:T(8,128)S(1)} %constant_dynamic-update-slice_fusion), kind=kOutput, calls=%fused_computation.1 | convolution fusion | flops 1749155840 | bytes 15728640 | tf_op jit(solution)/shard_map/dot_general | solution.py:207
  72.0 1.2 copy-done.2
  73.2 1.2 shard_map.58
  74.4 19.2 %all_to_all.32 = f32[8,16,512]{2,1,0:T(8,128)S(1)} all-to-all(f32[8,16,512]{2,1,0:T(8,128)S(1)} %broadcast_in_dim.16), channel_id=1, replica_groups=mesh['z'=8,'x'=4,'y'=4,'c'=2] {'z'}, dimensions={0} | all-to-all | bytes 524288 | tf_op jit(solution)/shard_map/all_to_all | solution.py:175
  93.8 13.5 %all_to_all.33 = f32[16,16,512]{2,1,0:T(8,128)S(1)} all-to-all(f32[16,16,512]{2,1,0:T(8,128)S(1)} %broadcast_in_dim.17), channel_id=1, replica_groups=mesh['z'=8,'x'=4,'y'=4,'c'=2] {'x','y'}, dimensions={0} | all-to-all | bytes 1048576 | tf_op jit(solution)/shard_map/all_to_all | solution.py:175
  107.3 1.9 %collective-permute-done.2 = f32[256,512]{1,0:T(8,128)S(1)} collective-permute-done((f32[256,512]{1,0:T(8,128)S(1)}, f32[256,512]{1,0:T(8,128)S(1)}, u32[]{:S(2)}, u32[]{:S(2)}) %collective-permute-start.2) | collective-permute-done | bytes 524320 | tf_op jit(solution)/shard_map/ppermute | solution.py:170
  109.4 18.7 %shard_map.59 = f32[512,512]{1,0:T(8,128)S(1)} custom-call(f32[512,512]{1,0:T(8,128)S(1)} %pad_maximum_fusion.gram_ref), custom_call_target="tpu_custom_call" | custom-call | flops 20000000000 | bytes 2097152 | tf_op jit(solution)/shard_map/pallas_call | solution.py:76
  128.2 2.9 %multiply_reduce_fusion = (f32[512]{0:T(512)S(1)}, bf16[208,512]{1,0:T(8,128)(2,1)}) fusion(f32[208,512]{1,0:T(8,128)} %reduce-scatter.2.cloned.1.call-done, f32[512,512]{1,0:T(8,128)S(1)} %shard_map.59), kind=kOutput, calls=%fused_computation.16 | convolution fusion | flops 654630400 | bytes 1689600 | tf_op jit(solution)/shard_map/dot_general | solution.py:216
  131.1 11.0 %all_to_all.34 = f32[32,4,128]{2,1,0:T(4,128)S(1)} all-to-all(f32[32,4,128]{2,1,0:T(4,128)S(1)} %broadcast_in_dim.19), channel_id=1, replica_groups=mesh['z'=8,'x'=4,'y'=4,'c'=2] {'x','y','c'}, dimensions={0} | all-to-all | bytes 131072 | tf_op jit(solution)/shard_map/all_to_all | solution.py:175
  142.2 0.6 broadcast_in_dim.40
  142.8 7.0 %all-to-all-start.5 = ((f32[8,4,128]{2,1,0:T(4,128)}), f32[8,4,128]{2,1,0:T(4,128)S(1)}, u32[]{:S(2)}, u32[]{:S(2)}) async-start(f32[8,4,128]{2,1,0:T(4,128)} %broadcast_in_dim.40), calls=%async_computation.6 | async-start | bytes 32768 | tf_op jit(solution)/shard_map/all_to_all | solution.py:175
  149.8 6.1 %convolution_convert_fusion.refs_0_ = bf16[1024,512]{1,0:T(8,128)(2,1)} fusion(f32[1024,512]{1,0:T(8,128)} %copy-done.3, f32[512,512]{1,0:T(8,128)S(1)} %shard_map.59), kind=kOutput, calls=%fused_computation.11 | convolution fusion | flops 3221749760 | bytes 4194304 | tf_op jit(solution)/shard_map/dot_general | solution.py:219
  155.9 0.6 reduce_sum.49
  156.5 10.7 %all-gather.2.cloned.1.call-done.refs_2_ = bf16[1664,512]{1,0:T(8,128)(2,1)} async-done(((bf16[208,512]{1,0:T(8,128)(2,1)}), bf16[1664,512]{1,0:T(8,128)(2,1)}) %all-gather.2.cloned.1.call-update) | async-done | bytes 1703952 | tf_op jit(solution)/shard_map/all_gather | solution.py:218
  167.2 8.1 %shard_map.60 = (bf16[1024,1664]{1,0:T(8,128)(2,1)}, bf16[1664,512]{1,0:T(8,128)(2,1)}, bf16[1024,1664]{1,0:T(8,128)(2,1)}) custom-call(bf16[1024,512]{1,0:T(8,128)(2,1)} %convolution_convert_fusion.refs_0_, bf16[1024,1664]{1,0:T(8,128)(2,1)} %copy-done.4, bf16[1664,512]{1,0:T(8,128)(2,1)} %all-gather.2.cloned.1.call-done.refs_2_, f32[1,512]{1,0:T(1,128)} %bitcast.24), custom_call_target="tpu_custom_call" | custom-call | flops 3489660928 | bytes 14680064 | tf_op jit(solution)/shard_map/pallas_call | solution.py:149
  (33 shorter events, 1.6 us)
Async XLA Ops:
  7.2 4.0 %copy-start = (bf16[1664,512]{1,0:T(8,128)(2,1)S(1)}, bf16[1664,512]{1,0:T(8,128)(2,1)}, u32[]{:S(2)}) copy-start(bf16[1664,512]{1,0:T(8,128)(2,1)} %param.5) | copy-start | bytes 5111812
  7.2 121.0 %reduce-scatter.2.cloned.1.call-start = ((), (), s32[]{:S(2)}) async-start(), calls=%async_computation.7 | async-start | bytes 3833856 | tf_op jit(solution)/shard_map/reduce_scatter | solution.py:209
  11.2 2.1 %copy-start.4 = (bf16[1024,1664]{1,0:T(8,128)(2,1)}, bf16[1024,1664]{1,0:T(8,128)(2,1)S(1)}, u32[]{:S(2)}) copy-start(bf16[1024,1664]{1,0:T(8,128)(2,1)S(1)} %add_convert_fusion.refs_1_) | copy-start | bytes 10223620
  13.3 2.9 %collective-permute-start = (f32[512,512]{1,0:T(8,128)}, f32[512,512]{1,0:T(8,128)S(1)}, u32[]{:S(2)}, u32[]{:S(2)}) collective-permute-start(f32[512,512]{1,0:T(8,128)} %fusion.1), channel_id=1, source_target_pairs={{0,1},{1,0},{2,3},{3,2},{4,5},{5,4},{6,7},{7,6},{8,9},{9,8},{10,11... | collective-permute-start | bytes 3145736 | tf_op jit(solution)/shard_map/ppermute | solution.py:170
  60.5 2.7 %collective-permute-start.1 = (f32[512,512]{1,0:T(8,128)S(1)}, f32[512,512]{1,0:T(8,128)S(1)}, u32[]{:S(2)}, u32[]{:S(2)}) collective-permute-start(f32[512,512]{1,0:T(8,128)S(1)} %bitcast.17), channel_id=1, source_target_pairs={{0,1},{1,0},{2,3},{3,2},{4,5},{5,4},{6,7},{7,6},{8,9},{9,8},{10,11... | collective-permute-start | bytes 3145736 | tf_op jit(solution)/shard_map/ppermute | solution.py:170
  60.8 3.5 %copy-start.5 = (bf16[1024,1664]{1,0:T(8,128)(2,1)S(1)}, bf16[1024,1664]{1,0:T(8,128)(2,1)}, u32[]{:S(2)}) copy-start(bf16[1024,1664]{1,0:T(8,128)(2,1)} %copy-done.4) | copy-start | bytes 10223620
  63.2 1.0 copy-start.1
  64.2 3.9 %copy-start.3 = (f32[1024,512]{1,0:T(8,128)}, f32[1024,512]{1,0:T(8,128)S(1)}, u32[]{:S(2)}) copy-start(f32[1024,512]{1,0:T(8,128)S(1)} %constant_dynamic-update-slice_fusion) | copy-start | bytes 6291460
  71.9 95.3 %all-gather.2.cloned.1.call-start = ((), (), s32[]{:S(2)}) async-start(), calls=%async_computation.8 | async-start | bytes 1916928 | tf_op jit(solution)/shard_map/all_gather | solution.py:218
  72.0 1.2 copy-start.2
  107.3 1.9 %collective-permute-start.2 = (f32[256,512]{1,0:T(8,128)S(1)}, f32[256,512]{1,0:T(8,128)S(1)}, u32[]{:S(2)}, u32[]{:S(2)}) collective-permute-start(f32[256,512]{1,0:T(8,128)S(1)} %bitcast.22), channel_id=1, source_target_pairs={{0,1},{1,0},{2,3},{3,2},{4,5},{5,4},{6,7},{7,6},{8,9},{9,8},{10,11... | collective-permute-start | bytes 1572872 | tf_op jit(solution)/shard_map/ppermute | solution.py:170
  142.8 13.1 %all-to-all-start.5 = ((f32[8,4,128]{2,1,0:T(4,128)}), f32[8,4,128]{2,1,0:T(4,128)S(1)}, u32[]{:S(2)}, u32[]{:S(2)}) async-start(f32[8,4,128]{2,1,0:T(4,128)} %broadcast_in_dim.40), calls=%async_computation.6 | async-start | bytes 32768 | tf_op jit(solution)/shard_map/all_to_all | solution.py:175
Sparse Core Ops, SparseCore 0:
  72.1 51.2 reduce-scatter.1
  131.2 35.9 all-gather.1
where the time goes:
time: 184 us; the launch traced here: 182 us
  blocking collectives  87.7 us (48%)
  Pallas kernels  28 us (15%)
  matrix products  21.3 us (12%)
  waiting for transfers between devices  15.3 us (8%)
  between operations  14.2 us (8%)
  starting transfers between devices  7.11 us (4%)
  other arithmetic  5.09 us (3%)
  local copies, waits for them, and re-layouts  3.42 us (2%)
    all_to_all x4, blocking collectives, spread_over(): return lax.all_to_all(many, axes, 0, 0, tiled=True)  63.4 us
    all_to_all x1, blocking collectives, per_device(): shard = jnp.sum(lax.all_to_all(pair, CHIPS, 0, 0, tiled=True), axis=0)  24.3 us
    pallas_call x1, Pallas kernels, chol_inverse(): pl.pallas_call(chol_kernel, out_shape=jax.ShapeDtypeStruct((n, n), jnp.fl...  18.7 us
    all_gather x1, waiting for transfers between devices, per_device(): lax.all_gather(right.astype(jnp.bfloat16), 'z', axis=0, tiled=True)  10.7 us
    pallas_call x1, Pallas kernels, last_products(): call(lambda *refs: last_kernel(factor, *refs), (big, jax.ShapeDtypeStruct...  8.13 us
    dot_general x3, matrix products, per_device(): lax.dot_general(blended, t, TN, preferred_element_type=jnp.float32)  7.68 us
    all_to_all x1, starting transfers between devices, spread_over(): return lax.all_to_all(many, axes, 0, 0, tiled=True)  7.03 us
    dot_general x1, matrix products, per_device(): lax.dot_general(left, inverse, NT, precision=HI, preferred_element_type=j...  6.07 us
  transfers between devices with their start and end apart: 6, of which 4 were waited for; matrix products, arithmetic and copies ran while one was open for 6% of the time, Pallas kernels for 11%

commit v1 on v0

--- a/solution.py
+++ b/solution.py
@@ -127,15 +127,20 @@
     )(place.reshape(1), left_a, left_b, left_a, left_b)
 
 
-def last_kernel(factor, orth_ref, blended_ref, right_ref, colsq_ref, momentum_ref, next_ref, update_ref):
-    @pl.when(pl.program_id(0) == 0)
+def last_kernel(factor, orth_ref, blended_ref, right_ref, colsq_ref, momentum_ref, next_ref, update_ref, scaled):
+    step = pl.program_id(0)
+
+    @pl.when(step == 0)
     def _():
         scale = 1.0 / jnp.sqrt(colsq_ref[...] + 1e-06)
-        next_ref[...] = (right_ref[...].astype(jnp.float32) * scale).astype(jnp.bfloat16)
+        scaled[...] = (right_ref[...].astype(jnp.float32) * scale).astype(jnp.bfloat16)
+
+    piece = next_ref.shape[0]
+    next_ref[...] = scaled[pl.ds(pl.multiple_of(step * piece, piece), piece), :]
 
     correction = lax.dot_general(orth_ref[...], right_ref[...], NT, preferred_element_type=jnp.float32)
     momentum_ref[...] = (blended_ref[...].astype(jnp.float32) - 0.1 * correction).astype(jnp.bfloat16)
-    product = lax.dot_general(orth_ref[...], next_ref[...], NT, preferred_element_type=jnp.float32)
+    product = lax.dot_general(orth_ref[...], scaled[...], NT, preferred_element_type=jnp.float32)
     update_ref[...] = (factor * product).astype(jnp.bfloat16)
 
 
@@ -151,7 +156,8 @@
         (big, jax.ShapeDtypeStruct((cols, rank), jnp.bfloat16), big),
         (rows // tile,),
         [pl.BlockSpec((tile, rank), lambda i: (i, 0)), block, whole, pl.BlockSpec((1, rank), lambda i: (0, 0))],
-        [block, whole, block],
+        [block, pl.BlockSpec((cols * tile // rows, rank), lambda i: (i, 0)), block],
+        [pltpu.VMEM((cols, rank), jnp.bfloat16)],
         flops=4 * rows * cols * rank,
         moved=6 * rows * cols + 4 * cols * rank + 2 * rows * rank,
         scalars=0,
@@ -203,11 +209,12 @@
     left_b = swap_cores(left_a)
     left = lax.dynamic_update_slice(jnp.zeros((rows_dev, rank), jnp.float32), left_a, (core * half, 0))
     left = lax.dynamic_update_slice(left, left_b, ((1 - core) * half, 0))
+    slab = gram_slab(place, rank // (2 * chips), left_a, left_b)
     wide = sum(
         lax.dot_general(blended, t, TN, preferred_element_type=jnp.float32) for t in three_terms(left)
     )
+    slab, wide = lax.optimization_barrier((slab, wide))
     wide = lax.psum_scatter(wide, "z", scatter_dimension=0, tiled=True)
-    slab = gram_slab(place, rank // (2 * chips), left_a, left_b)
     slab = jnp.sum(spread_over(slab, "z", depth), axis=0)
     mine = gather_over_chips(slab, chips)
     other = swap_cores(mine)

time: 184 us -> 184 us (level)
    unnamed x12 -> x8, local copies, waits for them, and re-layouts: 2.21 us -> 0.02 us
  transfers between devices with their start and end apart: 6 -> 6, of which waited for: 4 -> 4; matrix products, arithmetic and copies ran while one was open for 6% -> 6% of each run, Pallas kernels for 11% -> 10%
where the time goes in v1:
time: 184 us; the launch traced here: 182 us
  blocking collectives  86.2 us (47%)
  Pallas kernels  29.5 us (16%)
  matrix products  21.3 us (12%)
  waiting for transfers between devices  16 us (9%)
  between operations  14.2 us (8%)
  starting transfers between devices  6.73 us (4%)
  other arithmetic  5.09 us (3%)
  local copies, waits for them, and re-layouts  2.45 us (1%)
    all_to_all x4, blocking collectives, spread_over(): return lax.all_to_all(many, axes, 0, 0, tiled=True)  61.9 us
    all_to_all x1, blocking collectives, per_device(): shard = jnp.sum(lax.all_to_all(pair, CHIPS, 0, 0, tiled=True), axis=0)  24.3 us
    pallas_call x1, Pallas kernels, chol_inverse(): pl.pallas_call(chol_kernel, out_shape=jax.ShapeDtypeStruct((n, n), jnp.fl...  18.7 us
    all_gather x1, waiting for transfers between devices, per_device(): lax.all_gather(right.astype(jnp.bfloat16), 'z', axis=0, tiled=True)  11.3 us
    pallas_call x1, Pallas kernels, last_products(): call(lambda *refs: last_kernel(factor, *refs), (big, jax.ShapeDtypeStruct...  8.32 us
    dot_general x3, matrix products, per_device(): lax.dot_general(blended, t, TN, preferred_element_type=jnp.float32)  7.68 us
    all_to_all x1, starting transfers between devices, spread_over(): return lax.all_to_all(many, axes, 0, 0, tiled=True)  6.64 us
    dot_general x1, matrix products, per_device(): lax.dot_general(left, inverse, NT, precision=HI, preferred_element_type=j...  6.04 us
  transfers between devices with their start and end apart: 6, of which 4 were waited for; matrix products, arithmetic and copies ran while one was open for 6% of the time, Pallas kernels for 10%

profile of v1, /device:TPU:96, one launch (start us, length us, event | category | flops | bytes accessed | tf_op | source)
XLA Modules:
  0.0 181.5 jit_solution(7709297864054813298)
XLA Ops:
  7.2 3.9 %add_convert_fusion.refs_1_ = bf16[1024,1664]{1,0:T(8,128)(2,1)S(1)} fusion(bf16[1024,1664]{1,0:T(8,128)(2,1)} %param.3, bf16[1024,1664]{1,0:T(8,128)(2,1)} %param.4), kind=kLoop, calls=%fused_computation | loop fusion | flops 6815744 | bytes 10223616 | tf_op jit(solution)/shard_map/convert_element_type | solution.py:195
  11.2 2.1 %fusion.1 = f32[512,512]{1,0:T(8,128)} fusion(bf16[1664,512]{1,0:T(8,128)(2,1)S(1)} %copy-done, bf16[1024,1664]{1,0:T(8,128)(2,1)S(1)} %add_convert_fusion.refs_1_, s32[]{:T(128)S(6)} %select_n.21), kind=kOutput, calls=%fused_computation.7 | convolution fusion | flops 872415232 | bytes 4456452 | tf_op jit(solution)/shard_map/dot_general | solution.py:198
  13.3 2.6 %fusion.3 = f32[512,512]{1,0:T(8,128)S(1)} fusion(bf16[1664,512]{1,0:T(8,128)(2,1)S(1)} %copy-done, bf16[1024,1664]{1,0:T(8,128)(2,1)} %copy-done.2, s32[]{:T(128)S(6)} %select_n.20), kind=kOutput, calls=%fused_computation.9 | convolution fusion | flops 872415232 | bytes 4456452 | tf_op jit(solution)/shard_map/dot_general | solution.py:198
  15.9 0.3 collective-permute-done
  16.4 24.3 %all_to_all.30 = f32[16,32,512]{2,1,0:T(8,128)S(1)} all-to-all(f32[16,32,512]{2,1,0:T(8,128)S(1)} %bitcast.21), channel_id=1, replica_groups=mesh['z'=8,'x'=4,'y'=4,'c'=2] {'x','y'}, dimensions={0} | all-to-all | bytes 2097152 | tf_op jit(solution)/shard_map/all_to_all | solution.py:207
  40.9 19.6 %all_to_all.31 = f32[16,32,512]{2,1,0:T(8,128)S(1)} all-to-all(f32[16,32,512]{2,1,0:T(8,128)S(1)} %broadcast_in_dim.15), channel_id=1, replica_groups=mesh['z'=8,'x'=4,'y'=4,'c'=2] {'x','y'}, dimensions={0} | all-to-all | bytes 2097152 | tf_op jit(solution)/shard_map/all_to_all | solution.py:181
  60.9 2.4 %collective-permute-done.1.part_b.left_b = f32[512,512]{1,0:T(8,128)} collective-permute-done((f32[512,512]{1,0:T(8,128)S(1)}, f32[512,512]{1,0:T(8,128)}, u32[]{:S(2)}, u32[]{:S(2)}) %collective-permute-start.1) | collective-permute-done | bytes 1048608 | tf_op jit(solution)/shard_map/ppermute | solution.py:176
  63.3 1.3 constant_dynamic-update-slice_fusion
  64.6 2.0 %fusion.10 = f32[1664,512]{1,0:T(8,128)S(1)} fusion(bf16[1024,1664]{1,0:T(8,128)(2,1)S(1)} %copy-done.3, f32[1024,512]{1,0:T(8,128)S(1)} %constant_dynamic-update-slice_fusion), kind=kOutput, calls=%fused_computation.14 | convolution fusion | flops 1746927616 | bytes 8912896 | tf_op jit(solution)/shard_map/dot_general | solution.py:214
  66.6 2.0 %fusion.9 = f32[1664,512]{1,0:T(8,128)S(1)} fusion(bf16[1024,1664]{1,0:T(8,128)(2,1)S(1)} %copy-done.3, f32[1024,512]{1,0:T(8,128)S(1)} %constant_dynamic-update-slice_fusion), kind=kOutput, calls=%fused_computation.13 | convolution fusion | flops 1745879040 | bytes 8912896 | tf_op jit(solution)/shard_map/dot_general | solution.py:214
  68.6 3.8 %add_add_fusion = f32[1664,512]{1,0:T(8,128)} fusion(f32[1664,512]{1,0:T(8,128)S(1)} %fusion.9, f32[1664,512]{1,0:T(8,128)S(1)} %fusion.10, bf16[1024,1664]{1,0:T(8,128)(2,1)S(1)} %copy-done.3, f32[1024,512]{1,0:T(8,128)S(1)} %constant_dynamic-update-slice_fusion), kind=kOutput, calls=%fused_computation.1 | convolution fusion | flops 1749155840 | bytes 15728640 | tf_op jit(solution)/shard_map/dot_general | solution.py:214
  72.3 2.5 %shard_map.58 = f32[16,512]{1,0:T(8,128)S(1)} custom-call(s32[1]{0:T(128)} %bitcast.2.place_ref, f32[512,512]{1,0:T(8,128)S(1)} %bitcast.19, f32[512,512]{1,0:T(8,128)} %collective-permute-done.1.part_b.left_b, f32[512,512]{1,0:T(8,128)S(1)} %bitcast.20, f32[512,512]{1,0:T(8,128)} %collective-permute-done.1.part_b.left_b), custom_call_target="tpu_custom_call" | custom-call | flops 805306368 | bytes 2621440 | tf_op jit(solution)/shard_map/pallas_call | solution.py:118
  74.9 18.5 %all_to_all.32 = f32[8,16,512]{2,1,0:T(8,128)S(1)} all-to-all(f32[8,16,512]{2,1,0:T(8,128)S(1)} %broadcast_in_dim.16), channel_id=1, replica_groups=mesh['z'=8,'x'=4,'y'=4,'c'=2] {'z'}, dimensions={0} | all-to-all | bytes 524288 | tf_op jit(solution)/shard_map/all_to_all | solution.py:181
  93.5 12.7 %all_to_all.33 = f32[16,16,512]{2,1,0:T(8,128)S(1)} all-to-all(f32[16,16,512]{2,1,0:T(8,128)S(1)} %broadcast_in_dim.17), channel_id=1, replica_groups=mesh['z'=8,'x'=4,'y'=4,'c'=2] {'x','y'}, dimensions={0} | all-to-all | bytes 1048576 | tf_op jit(solution)/shard_map/all_to_all | solution.py:181
  106.2 1.9 %collective-permute-done.2 = f32[256,512]{1,0:T(8,128)S(1)} collective-permute-done((f32[256,512]{1,0:T(8,128)S(1)}, f32[256,512]{1,0:T(8,128)S(1)}, u32[]{:S(2)}, u32[]{:S(2)}) %collective-permute-start.2) | collective-permute-done | bytes 524320 | tf_op jit(solution)/shard_map/ppermute | solution.py:176
  108.4 18.7 %shard_map.59 = f32[512,512]{1,0:T(8,128)S(1)} custom-call(f32[512,512]{1,0:T(8,128)S(1)} %pad_maximum_fusion.gram_ref), custom_call_target="tpu_custom_call" | custom-call | flops 20000000000 | bytes 2097152 | tf_op jit(solution)/shard_map/pallas_call | solution.py:76
  127.1 2.9 %multiply_reduce_fusion = (f32[512]{0:T(512)S(1)}, bf16[208,512]{1,0:T(8,128)(2,1)}) fusion(f32[208,512]{1,0:T(8,128)} %reduce-scatter.2.cloned.1.call-done, f32[512,512]{1,0:T(8,128)S(1)} %shard_map.59), kind=kOutput, calls=%fused_computation.16 | convolution fusion | flops 654630400 | bytes 1689600 | tf_op jit(solution)/shard_map/dot_general | solution.py:223
  130.0 11.0 %all_to_all.34 = f32[32,4,128]{2,1,0:T(4,128)S(1)} all-to-all(f32[32,4,128]{2,1,0:T(4,128)S(1)} %broadcast_in_dim.19), channel_id=1, replica_groups=mesh['z'=8,'x'=4,'y'=4,'c'=2] {'x','y','c'}, dimensions={0} | all-to-all | bytes 131072 | tf_op jit(solution)/shard_map/all_to_all | solution.py:181
  141.1 0.6 broadcast_in_dim.40
  141.7 6.6 %all-to-all-start.5 = ((f32[8,4,128]{2,1,0:T(4,128)}), f32[8,4,128]{2,1,0:T(4,128)S(1)}, u32[]{:S(2)}, u32[]{:S(2)}) async-start(f32[8,4,128]{2,1,0:T(4,128)} %broadcast_in_dim.40), calls=%async_computation.6 | async-start | bytes 32768 | tf_op jit(solution)/shard_map/all_to_all | solution.py:181
  148.4 6.0 %convolution_convert_fusion.refs_0_ = bf16[1024,512]{1,0:T(8,128)(2,1)} fusion(f32[1024,512]{1,0:T(8,128)} %copy-done.1, f32[512,512]{1,0:T(8,128)S(1)} %shard_map.59), kind=kOutput, calls=%fused_computation.11 | convolution fusion | flops 3221749760 | bytes 4194304 | tf_op jit(solution)/shard_map/dot_general | solution.py:226
  154.4 0.6 reduce_sum.49
  155.1 11.3 %all-gather.2.cloned.1.call-done.refs_2_ = bf16[1664,512]{1,0:T(8,128)(2,1)} async-done(((bf16[208,512]{1,0:T(8,128)(2,1)}), bf16[1664,512]{1,0:T(8,128)(2,1)}) %all-gather.2.cloned.1.call-update) | async-done | bytes 1703952 | tf_op jit(solution)/shard_map/all_gather | solution.py:225
  166.4 8.3 %shard_map.60 = (bf16[1024,1664]{1,0:T(8,128)(2,1)}, bf16[1664,512]{1,0:T(8,128)(2,1)}, bf16[1024,1664]{1,0:T(8,128)(2,1)}) custom-call(bf16[1024,512]{1,0:T(8,128)(2,1)} %convolution_convert_fusion.refs_0_, bf16[1024,1664]{1,0:T(8,128)(2,1)} %copy-done.2, bf16[1664,512]{1,0:T(8,128)(2,1)} %all-gather.2.cloned.1.call-done.refs_2_, f32[1,512]{1,0:T(1,128)} %bitcast.24), custom_call_target="tpu_custom_call" | custom-call | flops 3489660928 | bytes 14680064 | tf_op jit(solution)/shard_map/pallas_call | solution.py:154
  (29 shorter events, 1.2 us)
Async XLA Ops:
  7.2 4.0 %copy-start = (bf16[1664,512]{1,0:T(8,128)(2,1)S(1)}, bf16[1664,512]{1,0:T(8,128)(2,1)}, u32[]{:S(2)}) copy-start(bf16[1664,512]{1,0:T(8,128)(2,1)} %param.5) | copy-start | bytes 5111812
  7.2 119.9 %reduce-scatter.2.cloned.1.call-start = ((), (), s32[]{:S(2)}) async-start(), calls=%async_computation.7 | async-start | bytes 3833856 | tf_op jit(solution)/shard_map/reduce_scatter | solution.py:217
  11.2 2.1 %copy-start.2 = (bf16[1024,1664]{1,0:T(8,128)(2,1)}, bf16[1024,1664]{1,0:T(8,128)(2,1)S(1)}, u32[]{:S(2)}) copy-start(bf16[1024,1664]{1,0:T(8,128)(2,1)S(1)} %add_convert_fusion.refs_1_) | copy-start | bytes 10223620
  13.3 2.9 %collective-permute-start = (f32[512,512]{1,0:T(8,128)}, f32[512,512]{1,0:T(8,128)S(1)}, u32[]{:S(2)}, u32[]{:S(2)}) collective-permute-start(f32[512,512]{1,0:T(8,128)} %fusion.1), channel_id=1, source_target_pairs={{0,1},{1,0},{2,3},{3,2},{4,5},{5,4},{6,7},{7,6},{8,9},{9,8},{10,11... | collective-permute-start | bytes 3145736 | tf_op jit(solution)/shard_map/ppermute | solution.py:176
  60.5 2.8 %collective-permute-start.1 = (f32[512,512]{1,0:T(8,128)S(1)}, f32[512,512]{1,0:T(8,128)}, u32[]{:S(2)}, u32[]{:S(2)}) collective-permute-start(f32[512,512]{1,0:T(8,128)S(1)} %bitcast.17), channel_id=1, source_target_pairs={{0,1},{1,0},{2,3},{3,2},{4,5},{5,4},{6,7},{7,6},{8,9},{9,8},{10,11... | collective-permute-start | bytes 3145736 | tf_op jit(solution)/shard_map/ppermute | solution.py:176
  60.8 3.8 %copy-start.3 = (bf16[1024,1664]{1,0:T(8,128)(2,1)S(1)}, bf16[1024,1664]{1,0:T(8,128)(2,1)}, u32[]{:S(2)}) copy-start(bf16[1024,1664]{1,0:T(8,128)(2,1)} %copy-done.2) | copy-start | bytes 10223620
  64.6 4.0 %copy-start.1 = (f32[1024,512]{1,0:T(8,128)}, f32[1024,512]{1,0:T(8,128)S(1)}, u32[]{:S(2)}) copy-start(f32[1024,512]{1,0:T(8,128)S(1)} %constant_dynamic-update-slice_fusion) | copy-start | bytes 6291460
  74.8 91.5 %all-gather.2.cloned.1.call-start = ((), (), s32[]{:S(2)}) async-start(), calls=%async_computation.8 | async-start | bytes 1916928 | tf_op jit(solution)/shard_map/all_gather | solution.py:225
  106.2 1.9 %collective-permute-start.2 = (f32[256,512]{1,0:T(8,128)S(1)}, f32[256,512]{1,0:T(8,128)S(1)}, u32[]{:S(2)}, u32[]{:S(2)}) collective-permute-start(f32[256,512]{1,0:T(8,128)S(1)} %bitcast.22), channel_id=1, source_target_pairs={{0,1},{1,0},{2,3},{3,2},{4,5},{5,4},{6,7},{7,6},{8,9},{9,8},{10,11... | collective-permute-start | bytes 1572872 | tf_op jit(solution)/shard_map/ppermute | solution.py:176
  141.7 12.7 %all-to-all-start.5 = ((f32[8,4,128]{2,1,0:T(4,128)}), f32[8,4,128]{2,1,0:T(4,128)S(1)}, u32[]{:S(2)}, u32[]{:S(2)}) async-start(f32[8,4,128]{2,1,0:T(4,128)} %broadcast_in_dim.40), calls=%async_computation.6 | async-start | bytes 32768 | tf_op jit(solution)/shard_map/all_to_all | solution.py:181
Sparse Core Ops, SparseCore 0:
  75.0 49.2 reduce-scatter.1
  130.1 36.1 all-gather.1

commit v2 on v1

--- a/solution.py
+++ b/solution.py
@@ -46,7 +46,8 @@
 def chol_kernel(gram_ref, inv_ref, work):
     n = gram_ref.shape[0]
     nb = 128
-    work[...] = gram_ref[...]
+    for r in range(0, n, nb):
+        work[r:r + nb, r:] = gram_ref[r:r + nb, r:]
     inv_ref[...] = jnp.zeros((n, n), jnp.float32)
     dot = lambda a, b: jnp.dot(a, b, precision=HI, preferred_element_type=jnp.float32)
 
@@ -59,7 +60,9 @@
         if after < n:
             u = dot(d, work[here, after:])
             ut = u.T
-            work[after:, after:] = work[after:, after:] - dot(ut, u)
+            for r in range(after, n, nb):
+                below = slice(r, r + nb)
+                work[below, r:] = work[below, r:] - dot(ut[r - after:r - after + nb, :], u[:, r - after:])
             inv_ref[after:, :after] = inv_ref[after:, :after] - dot(ut, inv_ref[here, :after])
 
     def step(k, carry):

time: 184 us -> 184 us (level)
  no operation moved by 1% of the time
where the time goes in v2:
time: 184 us; the launch traced here: 181 us
  blocking collectives  86.2 us (47%)
  Pallas kernels  29.3 us (16%)
  matrix products  21.3 us (12%)
  waiting for transfers between devices  16 us (9%)
  between operations  14.2 us (8%)
  starting transfers between devices  6.72 us (4%)
  other arithmetic  5.09 us (3%)
  local copies, waits for them, and re-layouts  2.45 us (1%)
    all_to_all x4, blocking collectives, spread_over(): return lax.all_to_all(many, axes, 0, 0, tiled=True)  61.9 us
    all_to_all x1, blocking collectives, per_device(): shard = jnp.sum(lax.all_to_all(pair, CHIPS, 0, 0, tiled=True), axis=0)  24.3 us
    pallas_call x1, Pallas kernels, chol_inverse(): pl.pallas_call(chol_kernel, out_shape=jax.ShapeDtypeStruct((n, n), jnp.fl...  18.5 us
    all_gather x1, waiting for transfers between devices, per_device(): lax.all_gather(right.astype(jnp.bfloat16), 'z', axis=0, tiled=True)  11.3 us
    pallas_call x1, Pallas kernels, last_products(): call(lambda *refs: last_kernel(factor, *refs), (big, jax.ShapeDtypeStruct...  8.32 us
    dot_general x3, matrix products, per_device(): lax.dot_general(blended, t, TN, preferred_element_type=jnp.float32)  7.68 us
    all_to_all x1, starting transfers between devices, spread_over(): return lax.all_to_all(many, axes, 0, 0, tiled=True)  6.63 us
    dot_general x1, matrix products, per_device(): lax.dot_general(left, inverse, NT, precision=HI, preferred_element_type=j...  6.05 us
  transfers between devices with their start and end apart: 6, of which 4 were waited for; matrix products, arithmetic and copies ran while one was open for 6% of the time, Pallas kernels for 10%

profile of v2, /device:TPU:96, one launch (start us, length us, event | category | flops | bytes accessed | tf_op | source)
XLA Modules:
  0.0 181.3 jit_solution(1353765014259979179)
XLA Ops:
  7.2 3.9 %add_convert_fusion.refs_1_ = bf16[1024,1664]{1,0:T(8,128)(2,1)S(1)} fusion(bf16[1024,1664]{1,0:T(8,128)(2,1)} %param.3, bf16[1024,1664]{1,0:T(8,128)(2,1)} %param.4), kind=kLoop, calls=%fused_computation | loop fusion | flops 6815744 | bytes 10223616 | tf_op jit(solution)/shard_map/convert_element_type | solution.py:198
  11.2 2.1 %fusion.1 = f32[512,512]{1,0:T(8,128)} fusion(bf16[1664,512]{1,0:T(8,128)(2,1)S(1)} %copy-done, bf16[1024,1664]{1,0:T(8,128)(2,1)S(1)} %add_convert_fusion.refs_1_, s32[]{:T(128)S(6)} %select_n.21), kind=kOutput, calls=%fused_computation.7 | convolution fusion | flops 872415232 | bytes 4456452 | tf_op jit(solution)/shard_map/dot_general | solution.py:201
  13.3 2.6 %fusion.3 = f32[512,512]{1,0:T(8,128)S(1)} fusion(bf16[1664,512]{1,0:T(8,128)(2,1)S(1)} %copy-done, bf16[1024,1664]{1,0:T(8,128)(2,1)} %copy-done.2, s32[]{:T(128)S(6)} %select_n.20), kind=kOutput, calls=%fused_computation.9 | convolution fusion | flops 872415232 | bytes 4456452 | tf_op jit(solution)/shard_map/dot_general | solution.py:201
  15.9 0.3 collective-permute-done
  16.4 24.3 %all_to_all.30 = f32[16,32,512]{2,1,0:T(8,128)S(1)} all-to-all(f32[16,32,512]{2,1,0:T(8,128)S(1)} %bitcast.21), channel_id=1, replica_groups=mesh['z'=8,'x'=4,'y'=4,'c'=2] {'x','y'}, dimensions={0} | all-to-all | bytes 2097152 | tf_op jit(solution)/shard_map/all_to_all | solution.py:210
  40.9 19.6 %all_to_all.31 = f32[16,32,512]{2,1,0:T(8,128)S(1)} all-to-all(f32[16,32,512]{2,1,0:T(8,128)S(1)} %broadcast_in_dim.15), channel_id=1, replica_groups=mesh['z'=8,'x'=4,'y'=4,'c'=2] {'x','y'}, dimensions={0} | all-to-all | bytes 2097152 | tf_op jit(solution)/shard_map/all_to_all | solution.py:184
  60.9 2.4 %collective-permute-done.1.part_b.left_b = f32[512,512]{1,0:T(8,128)} collective-permute-done((f32[512,512]{1,0:T(8,128)S(1)}, f32[512,512]{1,0:T(8,128)}, u32[]{:S(2)}, u32[]{:S(2)}) %collective-permute-start.1) | collective-permute-done | bytes 1048608 | tf_op jit(solution)/shard_map/ppermute | solution.py:179
  63.3 1.3 constant_dynamic-update-slice_fusion
  64.6 2.0 %fusion.10 = f32[1664,512]{1,0:T(8,128)S(1)} fusion(bf16[1024,1664]{1,0:T(8,128)(2,1)S(1)} %copy-done.3, f32[1024,512]{1,0:T(8,128)S(1)} %constant_dynamic-update-slice_fusion), kind=kOutput, calls=%fused_computation.14 | convolution fusion | flops 1746927616 | bytes 8912896 | tf_op jit(solution)/shard_map/dot_general | solution.py:217
  66.6 2.0 %fusion.9 = f32[1664,512]{1,0:T(8,128)S(1)} fusion(bf16[1024,1664]{1,0:T(8,128)(2,1)S(1)} %copy-done.3, f32[1024,512]{1,0:T(8,128)S(1)} %constant_dynamic-update-slice_fusion), kind=kOutput, calls=%fused_computation.13 | convolution fusion | flops 1745879040 | bytes 8912896 | tf_op jit(solution)/shard_map/dot_general | solution.py:217
  68.6 3.8 %add_add_fusion = f32[1664,512]{1,0:T(8,128)} fusion(f32[1664,512]{1,0:T(8,128)S(1)} %fusion.9, f32[1664,512]{1,0:T(8,128)S(1)} %fusion.10, bf16[1024,1664]{1,0:T(8,128)(2,1)S(1)} %copy-done.3, f32[1024,512]{1,0:T(8,128)S(1)} %constant_dynamic-update-slice_fusion), kind=kOutput, calls=%fused_computation.1 | convolution fusion | flops 1749155840 | bytes 15728640 | tf_op jit(solution)/shard_map/dot_general | solution.py:217
  72.3 2.5 %shard_map.58 = f32[16,512]{1,0:T(8,128)S(1)} custom-call(s32[1]{0:T(128)} %bitcast.2.place_ref, f32[512,512]{1,0:T(8,128)S(1)} %bitcast.19, f32[512,512]{1,0:T(8,128)} %collective-permute-done.1.part_b.left_b, f32[512,512]{1,0:T(8,128)S(1)} %bitcast.20, f32[512,512]{1,0:T(8,128)} %collective-permute-done.1.part_b.left_b), custom_call_target="tpu_custom_call" | custom-call | flops 805306368 | bytes 2621440 | tf_op jit(solution)/shard_map/pallas_call | solution.py:121
  74.9 18.5 %all_to_all.32 = f32[8,16,512]{2,1,0:T(8,128)S(1)} all-to-all(f32[8,16,512]{2,1,0:T(8,128)S(1)} %broadcast_in_dim.16), channel_id=1, replica_groups=mesh['z'=8,'x'=4,'y'=4,'c'=2] {'z'}, dimensions={0} | all-to-all | bytes 524288 | tf_op jit(solution)/shard_map/all_to_all | solution.py:184
  93.5 12.7 %all_to_all.33 = f32[16,16,512]{2,1,0:T(8,128)S(1)} all-to-all(f32[16,16,512]{2,1,0:T(8,128)S(1)} %broadcast_in_dim.17), channel_id=1, replica_groups=mesh['z'=8,'x'=4,'y'=4,'c'=2] {'x','y'}, dimensions={0} | all-to-all | bytes 1048576 | tf_op jit(solution)/shard_map/all_to_all | solution.py:184
  106.2 1.9 %collective-permute-done.2 = f32[256,512]{1,0:T(8,128)S(1)} collective-permute-done((f32[256,512]{1,0:T(8,128)S(1)}, f32[256,512]{1,0:T(8,128)S(1)}, u32[]{:S(2)}, u32[]{:S(2)}) %collective-permute-start.2) | collective-permute-done | bytes 524320 | tf_op jit(solution)/shard_map/ppermute | solution.py:179
  108.4 18.5 %shard_map.59 = f32[512,512]{1,0:T(8,128)S(1)} custom-call(f32[512,512]{1,0:T(8,128)S(1)} %pad_maximum_fusion.gram_ref), custom_call_target="tpu_custom_call" | custom-call | flops 20000000000 | bytes 2097152 | tf_op jit(solution)/shard_map/pallas_call | solution.py:79
  126.9 2.9 %multiply_reduce_fusion = (f32[512]{0:T(512)S(1)}, bf16[208,512]{1,0:T(8,128)(2,1)}) fusion(f32[208,512]{1,0:T(8,128)} %reduce-scatter.2.cloned.1.call-done, f32[512,512]{1,0:T(8,128)S(1)} %shard_map.59), kind=kOutput, calls=%fused_computation.16 | convolution fusion | flops 654630400 | bytes 1689600 | tf_op jit(solution)/shard_map/dot_general | solution.py:226
  129.8 11.1 %all_to_all.34 = f32[32,4,128]{2,1,0:T(4,128)S(1)} all-to-all(f32[32,4,128]{2,1,0:T(4,128)S(1)} %broadcast_in_dim.19), channel_id=1, replica_groups=mesh['z'=8,'x'=4,'y'=4,'c'=2] {'x','y','c'}, dimensions={0} | all-to-all | bytes 131072 | tf_op jit(solution)/shard_map/all_to_all | solution.py:184
  140.9 0.6 broadcast_in_dim.40
  141.5 6.6 %all-to-all-start.5 = ((f32[8,4,128]{2,1,0:T(4,128)}), f32[8,4,128]{2,1,0:T(4,128)S(1)}, u32[]{:S(2)}, u32[]{:S(2)}) async-start(f32[8,4,128]{2,1,0:T(4,128)} %broadcast_in_dim.40), calls=%async_computation.6 | async-start | bytes 32768 | tf_op jit(solution)/shard_map/all_to_all | solution.py:184
  148.2 6.0 %convolution_convert_fusion.refs_0_ = bf16[1024,512]{1,0:T(8,128)(2,1)} fusion(f32[1024,512]{1,0:T(8,128)} %copy-done.1, f32[512,512]{1,0:T(8,128)S(1)} %shard_map.59), kind=kOutput, calls=%fused_computation.11 | convolution fusion | flops 3221749760 | bytes 4194304 | tf_op jit(solution)/shard_map/dot_general | solution.py:229
  154.2 0.6 reduce_sum.49
  154.8 11.3 %all-gather.2.cloned.1.call-done.refs_2_ = bf16[1664,512]{1,0:T(8,128)(2,1)} async-done(((bf16[208,512]{1,0:T(8,128)(2,1)}), bf16[1664,512]{1,0:T(8,128)(2,1)}) %all-gather.2.cloned.1.call-update) | async-done | bytes 1703952 | tf_op jit(solution)/shard_map/all_gather | solution.py:228
  166.2 8.3 %shard_map.60 = (bf16[1024,1664]{1,0:T(8,128)(2,1)}, bf16[1664,512]{1,0:T(8,128)(2,1)}, bf16[1024,1664]{1,0:T(8,128)(2,1)}) custom-call(bf16[1024,512]{1,0:T(8,128)(2,1)} %convolution_convert_fusion.refs_0_, bf16[1024,1664]{1,0:T(8,128)(2,1)} %copy-done.2, bf16[1664,512]{1,0:T(8,128)(2,1)} %all-gather.2.cloned.1.call-done.refs_2_, f32[1,512]{1,0:T(1,128)} %bitcast.24), custom_call_target="tpu_custom_call" | custom-call | flops 3489660928 | bytes 14680064 | tf_op jit(solution)/shard_map/pallas_call | solution.py:157
  (29 shorter events, 1.2 us)
Async XLA Ops:
  7.2 4.0 %copy-start = (bf16[1664,512]{1,0:T(8,128)(2,1)S(1)}, bf16[1664,512]{1,0:T(8,128)(2,1)}, u32[]{:S(2)}) copy-start(bf16[1664,512]{1,0:T(8,128)(2,1)} %param.5) | copy-start | bytes 5111812
  7.2 119.7 %reduce-scatter.2.cloned.1.call-start = ((), (), s32[]{:S(2)}) async-start(), calls=%async_computation.7 | async-start | bytes 3833856 | tf_op jit(solution)/shard_map/reduce_scatter | solution.py:220
  11.2 2.1 %copy-start.2 = (bf16[1024,1664]{1,0:T(8,128)(2,1)}, bf16[1024,1664]{1,0:T(8,128)(2,1)S(1)}, u32[]{:S(2)}) copy-start(bf16[1024,1664]{1,0:T(8,128)(2,1)S(1)} %add_convert_fusion.refs_1_) | copy-start | bytes 10223620
  13.3 2.9 %collective-permute-start = (f32[512,512]{1,0:T(8,128)}, f32[512,512]{1,0:T(8,128)S(1)}, u32[]{:S(2)}, u32[]{:S(2)}) collective-permute-start(f32[512,512]{1,0:T(8,128)} %fusion.1), channel_id=1, source_target_pairs={{0,1},{1,0},{2,3},{3,2},{4,5},{5,4},{6,7},{7,6},{8,9},{9,8},{10,11... | collective-permute-start | bytes 3145736 | tf_op jit(solution)/shard_map/ppermute | solution.py:179
  60.5 2.8 %collective-permute-start.1 = (f32[512,512]{1,0:T(8,128)S(1)}, f32[512,512]{1,0:T(8,128)}, u32[]{:S(2)}, u32[]{:S(2)}) collective-permute-start(f32[512,512]{1,0:T(8,128)S(1)} %bitcast.17), channel_id=1, source_target_pairs={{0,1},{1,0},{2,3},{3,2},{4,5},{5,4},{6,7},{7,6},{8,9},{9,8},{10,11... | collective-permute-start | bytes 3145736 | tf_op jit(solution)/shard_map/ppermute | solution.py:179
  60.8 3.8 %copy-start.3 = (bf16[1024,1664]{1,0:T(8,128)(2,1)S(1)}, bf16[1024,1664]{1,0:T(8,128)(2,1)}, u32[]{:S(2)}) copy-start(bf16[1024,1664]{1,0:T(8,128)(2,1)} %copy-done.2) | copy-start | bytes 10223620
  64.6 4.0 %copy-start.1 = (f32[1024,512]{1,0:T(8,128)}, f32[1024,512]{1,0:T(8,128)S(1)}, u32[]{:S(2)}) copy-start(f32[1024,512]{1,0:T(8,128)S(1)} %constant_dynamic-update-slice_fusion) | copy-start | bytes 6291460
  74.8 91.3 %all-gather.2.cloned.1.call-start = ((), (), s32[]{:S(2)}) async-start(), calls=%async_computation.8 | async-start | bytes 1916928 | tf_op jit(solution)/shard_map/all_gather | solution.py:228
  106.2 1.9 %collective-permute-start.2 = (f32[256,512]{1,0:T(8,128)S(1)}, f32[256,512]{1,0:T(8,128)S(1)}, u32[]{:S(2)}, u32[]{:S(2)}) collective-permute-start(f32[256,512]{1,0:T(8,128)S(1)} %bitcast.22), channel_id=1, source_target_pairs={{0,1},{1,0},{2,3},{3,2},{4,5},{5,4},{6,7},{7,6},{8,9},{9,8},{10,11... | collective-permute-start | bytes 1572872 | tf_op jit(solution)/shard_map/ppermute | solution.py:179
  141.5 12.7 %all-to-all-start.5 = ((f32[8,4,128]{2,1,0:T(4,128)}), f32[8,4,128]{2,1,0:T(4,128)S(1)}, u32[]{:S(2)}, u32[]{:S(2)}) async-start(f32[8,4,128]{2,1,0:T(4,128)} %broadcast_in_dim.40), calls=%async_computation.6 | async-start | bytes 32768 | tf_op jit(solution)/shard_map/all_to_all | solution.py:184
Sparse Core Ops, SparseCore 0:
  75.0 49.2 reduce-scatter.1
  129.9 36.1 all-gather.1
